TPU v7x, 32 devices: a whole 2x2x4 slice. The times are simulated.
32 devices in a mesh: groups: 2 (over y), dp: 4 (over x, core), tensor: 4 (over z).
Axes of the slice: x: 2, y: 2, z: 4, core: 2. Of those that a mesh axis runs over, the one named last changes fastest.
Arguments:
- tokens: bfloat16 [8192, 8192], P(('groups', 'dp'), 'tensor'), parts along dimension 0, may hold values from -6 to 6
- key_value_weight: bfloat16 [8192, 2048], P('tensor'), may hold values from -0.0625 to 0.0625
- adapter_down_factors: bfloat16 [48, 8192, 64], P(('groups', 'dp'), 'tensor'), parts along dimension 0, may hold values from -0.0625 to 0.0625
- adapter_up_factors: bfloat16 [48, 64, 2048], P(('groups', 'dp'), None, 'tensor'), parts along dimension 0, may hold values from -0.375 to 0.375
- adapter_per_block: int32 [64], P('groups'), parts along dimension 0, may hold values from 0 to 23, as said below
- live_rows_per_block: int32 [64], P(('groups', 'dp')), parts along dimension 0, may hold values from 1 to 128, as said below
- adapter_storage_slot: int32 [48], P('groups'), parts along dimension 0, may hold values from 0 to 23, each once
Outputs:
- keys_values: bfloat16 [8192, 2048], P(('groups', 'dp'), 'tensor'), parts along dimension 0
There are 2 independent parts, one for each index of `groups`. A program takes and returns all parts, laid end to end along the dimension named above; an argument that names none is the same for every part. Nothing has to cross between parts.
Inputs may be any that keep to these rules, and one draw needn't show every extreme that they name: `adapter_per_block`: the blocks of one adapter stand together; one adapter holds exactly 6 blocks, every other used one 1 to 3; about half as many adapters as blocks are used. `live_rows_per_block`: every block of an adapter is full but its last one.
All inputs are finite; a program needn't handle non-finite values.
Results may differ from a plain program's by a relative error of at most 0.001.
Values may be sent and summed in bfloat16 or wider, within the bound.
A program may use at most 128 MiB of HBM per device.

v0:
```python
import jax
import jax.numpy as jnp
from jax import lax
from jax.sharding import PartitionSpec as P

ADAPTER_SCALE = 2.0


def on_device(
    tokens,
    key_value_weight,
    adapter_down_factors,
    adapter_up_factors,
    adapter_per_block,
    live_rows_per_block,
    adapter_storage_slot,
):
    blocks_here = live_rows_per_block.shape[0]
    tok_rows = tokens.shape[0]
    width_here = tokens.shape[1]
    block_length = tok_rows // blocks_here
    adapter_rank_width = adapter_down_factors.shape[2]
    output_width = adapter_up_factors.shape[2]
    position = lax.axis_index("dp")
    every_slot = adapter_storage_slot[adapter_per_block]
    my_slots = lax.dynamic_slice_in_dim(every_slot, position * blocks_here, blocks_here)
    starting = (
        jnp.zeros((blocks_here, width_here, adapter_rank_width), jnp.bfloat16),
        jnp.zeros((blocks_here, adapter_rank_width, output_width), jnp.bfloat16),
    )
    pieces = (
        lax.all_gather(adapter_down_factors, "dp", axis=0, tiled=True),
        lax.all_gather(adapter_up_factors, "dp", axis=0, tiled=True),
    )
    piece_count = pieces[0].shape[0]
    inside = (my_slots >= 0) & (my_slots < piece_count)
    piece_index = jnp.clip(my_slots, 0, piece_count - 1)
    fresh_down_factor = jnp.where(inside[:, None, None], pieces[0][piece_index], starting[0])
    up_new = jnp.where(inside[:, None, None], pieces[1][piece_index], starting[1])
    blocked_tokens = tokens.reshape(blocks_here, block_length, width_here)
    lowrank_output = jnp.einsum(
        "zlq,zqg->zlg", blocked_tokens, fresh_down_factor, preferred_element_type=jnp.float32
    )
    base_output = jnp.dot(tokens, key_value_weight, preferred_element_type=jnp.float32)
    low_whole = lax.psum(lowrank_output, "tensor")
    adapter_term = jnp.einsum(
        "bkr,brc->bkc", low_whole, up_new.astype(jnp.float32), precision=lax.Precision.HIGHEST
    ).reshape(tok_rows, output_width)
    combined_output = lax.psum_scatter(base_output, "tensor", scatter_dimension=1, tiled=True)
    combined_output = combined_output + ADAPTER_SCALE * adapter_term
    live_rows = jnp.arange(block_length)[None, :] < live_rows_per_block[:, None]
    result = jnp.where(live_rows.reshape(tok_rows)[:, None], combined_output, jnp.float32(0.0))
    return result.astype(jnp.bfloat16)


def solution(mesh):
    placed = (
        P(("groups", "dp"), "tensor"),
        P("tensor", None),
        P(("groups", "dp"), "tensor", None),
        P(("groups", "dp"), None, "tensor"),
        P("groups"),
        P(("groups", "dp")),
        P("groups"),
    )
    return jax.shard_map(
        on_device,
        mesh=mesh,
        in_specs=placed,
        out_specs=P(("groups", "dp"), "tensor"),
        check_vma=False,
    )
```

profile of v0, /device:TPU:0, one launch (start us, length us, event | category | flops | bytes accessed | tf_op | source)
XLA Modules:
  0.0 273.0 jit_solution(5887742405895497234)
XLA Ops:
  6.5 0.0 copy-start
  6.5 0.0 all-gather.3.cloned.1.call-start
  6.5 0.7 all-gather.3.cloned.1.call-update
  7.3 0.0 all-gather.5.cloned.1.call-start
  7.3 0.7 all-gather.5.cloned.1.call-update
  8.0 0.0 all-reduce.2.cloned.1.call-start
  8.1 0.7 compare_select_fusion.1
  8.7 0.0 copy-done
  8.7 0.7 gather_fusion
  9.4 0.1 compare_select_fusion
  9.5 0.1 compare_and_fusion
  9.6 48.4 %all-gather.3.cloned.1.call-done = bf16[24,2048,64]{1,2,0:T(8,128)(2,1)} async-done(((bf16[6,2048,64]{1,2,0:T(8,128)(2,1)}), bf16[24,2048,64]{1,2,0:T(8,128)(2,1)}) %all-gather.3.cloned.1.call-update) | async-done | bytes 6291472 | tf_op jit(solution)/shard_map/all_gather | solution.py:32
  58.0 3.5 %gather_fusion.1 = bf16[8,2048,64]{1,2,0:T(8,128)(2,1)S(1)} fusion(bf16[24,2048,64]{1,2,0:T(8,128)(2,1)} %all-gather.3.cloned.1.call-done, s32[1024]{0:T(1024)S(1)} %pad_clamp_fusion), kind=kCustom, calls=%fused_computation.1 | custom fusion | bytes 4194336 | tf_op jit(solution)/shard_map/gather | solution.py:38
  61.5 4.5 %fusion.5 = f32[8,128,64]{1,2,0:T(8,128)} fusion(bf16[8,128,2048]{2,1,0:T(8,128)(2,1)} %bitcast.15, bf16[8,2048,64]{1,2,0:T(8,128)(2,1)S(1)} %gather_fusion.1, pred[8]{0:T(512)(128)(4,1)S(1)} %compare_and_fusion), kind=kOutput, calls=%fused_computation.10 | convolution fusion | flops 269484032 | bytes 6553608 | tf_op jit(solution)/shard_map/zlq,zqg->zlg/dot_general | solution.py:41
  66.0 0.0 all-reduce.2.cloned.1.call-update
  66.1 0.0 reduce-scatter.2.cloned.1.call-start
  66.1 14.8 %fusion.15 = f32[1024,2048]{1,0:T(8,128)} fusion(bf16[1024,2048]{1,0:T(8,128)(2,1)} %param.7, bf16[2048,2048]{1,0:T(8,128)(2,1)} %param.8), kind=kOutput, calls=%fused_computation.24 | convolution fusion | flops 8589934592 | bytes 20971520 | tf_op jit(solution)/shard_map/dot_general | solution.py:44
  80.9 0.0 copy-start.1
  80.9 0.0 reduce-scatter.2.cloned.1.call-update
  81.0 0.6 copy-done.1
  81.6 0.1 fusion.12
  81.7 0.0 all-gather.5.cloned.1.call-done
  81.7 2.0 gather_fusion.2
  83.7 33.3 %all-reduce.2.cloned.1.call-done = f32[8,128,64]{1,2,0:T(8,128)} async-done(((f32[8,128,64]{1,2,0:T(8,128)}), f32[8,128,64]{1,2,0:T(8,128)}) %all-reduce.2.cloned.1.call-update) | async-done | bytes 262160 | tf_op jit(solution)/shard_map/psum | solution.py:45
  117.0 2.0 convolution_multiply_fusion
  119.0 144.6 %reduce-scatter.2.cloned.1.call-done = f32[1024,512]{1,0:T(8,128)} async-done(((f32[1024,2048]{1,0:T(8,128)}), f32[1024,512]{1,0:T(8,128)}) %reduce-scatter.2.cloned.1.call-update) | async-done | bytes 2097168 | tf_op jit(solution)/shard_map/reduce_scatter | solution.py:49
  263.6 2.9 %fusion.1 = bf16[1024,512]{1,0:T(8,128)(2,1)} fusion(f32[1024,512]{1,0:T(8,128)} %reduce-scatter.2.cloned.1.call-done, f32[8,128,512]{2,1,0:T(8,128)S(1)} %convolution_multiply_fusion, pred[1024]{0:T(1024)(128)(4,1)S(1)} %fusion.12), kind=kLoop, calls=%fused_computation.5 | loop fusion | flops 1572864 | bytes 5243904 | tf_op jit(solution)/shard_map/convert_element_type | solution.py:53
  (2 shorter events, 0.0 us)
Async XLA Ops:
  6.5 2.2 copy-start
  6.5 51.5 %all-gather.3.cloned.1.call-start = ((), (), s32[]{:S(2)}) async-start(), calls=%async_computation.2 | async-start | bytes 7864320 | tf_op jit(solution)/shard_map/all_gather | solution.py:32
  7.3 74.4 %all-gather.5.cloned.1.call-start = ((), (), s32[]{:S(2)}) async-start(), calls=%async_computation.4 | async-start | bytes 1966080 | tf_op jit(solution)/shard_map/all_gather | solution.py:33
  8.0 109.0 %all-reduce.2.cloned.1.call-start = ((), (), s32[]{:S(2)}) async-start(), calls=%async_computation.3 | async-start | bytes 524288 | tf_op jit(solution)/shard_map/psum | solution.py:45
  66.1 197.5 %reduce-scatter.2.cloned.1.call-start = ((), (), s32[]{:S(2)}) async-start(), calls=%async_computation.1 | async-start | bytes 10485760 | tf_op jit(solution)/shard_map/reduce_scatter | solution.py:49
  80.9 0.7 copy-start.1
Sparse Core Ops, SparseCore 0:
  8.9 49.0 all-gather.2
  59.6 19.6 all-gather.4
  81.6 35.3 all-reduce.1
  119.3 144.2 reduce-scatter.1
where the time goes:
time: 273 us
  waiting for transfers between devices  228 us (84%)
  matrix products  21.4 us (8%)
  between operations  13.2 us (5%)
  local copies, waits for them, and re-layouts  6.78 us (2%)
  other arithmetic  3.76 us (1%)
    reduce_scatter x1, waiting for transfers between devices, on_device(): lax.psum_scatter(base_output, 'tensor', scatter_dimension=1, tiled=True)  145 us
    all_gather x1, waiting for transfers between devices, on_device(): lax.all_gather(adapter_down_factors, 'dp', axis=0, tiled=True)  48.4 us
    psum x1, waiting for transfers between devices, on_device(): low_whole = lax.psum(lowrank_output, 'tensor')  33.3 us
    dot_general x1, matrix products, on_device(): jnp.dot(tokens, key_value_weight, preferred_element_type=jnp.float32)  14.8 us
  transfers between devices with their start and end apart: 4, of which 3 were waited for; matrix products, arithmetic and copies ran while one was open for 10% of the time, Pallas kernels for 0%

commit v1 on v0

v1 whole, which is shorter than its diff:
```python
import functools

import jax
import jax.numpy as jnp
from jax import lax
from jax.experimental import pallas as pl
from jax.experimental.pallas import tpu as pltpu
from jax.sharding import PartitionSpec as P

ADAPTER_SCALE = 2.0
MESH = pl.DeviceIdType.MESH
F32 = jnp.float32
LEVELS = 32767.0


def kernel(
    T, X, R, NB, BL,
    apb, slot_of, live, tok_h, w_h, dn_h, up_h, out,
    tok, w, dn, up, acc, low,
    su, sd, ru, rd, ssu, ssd, rsu, rsd,
    lsu, lsd, lru, lrd,
    sem_tok, sem_w, sem_own,
    s_u, s_d, r_u, r_d, s_us, s_ds, r_us, r_ds,
    s_low, r_low, s_x, r_x, s_c, r_c,
):
    RB = tok.shape[0] // R
    AP = dn_h.shape[0]
    t = lax.axis_index("tensor")
    pos = lax.axis_index("dp")
    x, core = pos // 2, pos % 2
    right = lax.rem(x + 1, X) * 2 + core
    left = lax.rem(x + X - 1, X) * 2 + core
    partner = x * 2 + 1 - core
    has_lo, has_hi = t > 0, t < T - 1

    def rows(r):
        return pl.ds(pl.multiple_of(r * RB, RB), RB)

    N = w_h.shape[1] // T
    order = []
    for p in range((T + 1) // 2):
        for d in (T - 1 - p, p):
            if d not in order:
                order.append(d)

    def w_copy(d):
        return pltpu.make_async_copy(w_h.at[:, d * N:(d + 1) * N], w.at[d], sem_w.at[d])

    def tok_copy(r):
        return pltpu.make_async_copy(tok_h.at[rows(r)], tok.at[rows(r)], sem_tok.at[r])

    w_copy(order[0]).start()
    tok_copy(0).start()
    w_copy(order[1]).start()
    for r in range(1, R):
        tok_copy(r).start()
    for d in order[2:]:
        w_copy(d).start()

    def piece(ref, owner):
        return ref.at[pl.ds(owner * AP, AP)]

    own_dn = pltpu.make_async_copy(dn_h, piece(dn, pos), sem_own.at[0])
    own_up = pltpu.make_async_copy(up_h, piece(up, pos), sem_own.at[1])
    own_dn.start()
    own_up.start()

    bar = pltpu.get_barrier_semaphore()

    @pl.when(has_lo)
    def _():
        pl.semaphore_signal(bar, inc=1, device_id={"tensor": t - 1}, device_id_type=MESH)

    @pl.when(has_hi)
    def _():
        pl.semaphore_signal(bar, inc=1, device_id={"tensor": t + 1}, device_id_type=MESH)

    peers = [partner]
    if X > 1:
        peers.append(right)
    if X > 2:
        peers.append(left)
    for q in peers:
        pl.semaphore_signal(bar, inc=1, device_id={"dp": q}, device_id_type=MESH)
    pl.semaphore_wait(bar, has_lo.astype(jnp.int32) + has_hi.astype(jnp.int32) + len(peers))

    def x_copy(s, k):
        owner = lax.rem(x - s + X, X) * 2 + core
        full, mine = (dn, dn_h) if k == 0 else (up, up_h)
        return pltpu.make_async_remote_copy(
            src_ref=mine if s == 0 else piece(full, owner), dst_ref=piece(full, owner),
            send_sem=s_x.at[s, k], recv_sem=r_x.at[s, k],
            device_id={"dp": right}, device_id_type=MESH)

    def c_copy(s, k):
        owner = lax.rem(x - s + X, X) * 2 + core
        full, mine = (dn, dn_h) if k == 0 else (up, up_h)
        return pltpu.make_async_remote_copy(
            src_ref=mine if s == 0 else piece(full, owner), dst_ref=piece(full, owner),
            send_sem=s_c.at[s, k], recv_sem=r_c.at[s, k],
            device_id={"dp": partner}, device_id_type=MESH)

    if X > 1:
        for k in range(2):
            x_copy(0, k).start()
    for k in range(2):
        c_copy(0, k).start()

    def u_copy(i, r):
        return (
            pltpu.make_async_remote_copy(
                src_ref=su.at[i, rows(r)], dst_ref=ru.at[i, rows(r)], send_sem=s_u.at[i, r],
                recv_sem=r_u.at[i, r], device_id={"tensor": t + 1}, device_id_type=MESH),
            pltpu.make_async_remote_copy(
                src_ref=ssu.at[i, r], dst_ref=rsu.at[i, r], send_sem=s_us.at[i, r],
                recv_sem=r_us.at[i, r], device_id={"tensor": t + 1}, device_id_type=MESH),
        )

    def d_copy(i, r):
        return (
            pltpu.make_async_remote_copy(
                src_ref=sd.at[i, rows(r)], dst_ref=rd.at[i, rows(r)], send_sem=s_d.at[i, r],
                recv_sem=r_d.at[i, r], device_id={"tensor": t - 1}, device_id_type=MESH),
            pltpu.make_async_remote_copy(
                src_ref=ssd.at[i, r], dst_ref=rsd.at[i, r], send_sem=s_ds.at[i, r],
                recv_sem=r_ds.at[i, r], device_id={"tensor": t - 1}, device_id_type=MESH),
        )

    def product(d, r):
        return jnp.dot(tok[rows(r), :], w[d], preferred_element_type=F32)

    def encode(v, q_ref, s_ref, i, r):
        top = jnp.maximum(jnp.max(jnp.abs(v), axis=0, keepdims=True), 1e-30)
        q_ref[i, rows(r), :] = jnp.round(v * (LEVELS / top)).astype(jnp.int32).astype(jnp.int16)
        s_ref[i, r] = top * (1.0 / LEVELS)

    def decode(q_ref, s_ref, i, r):
        return q_ref[i, rows(r), :].astype(jnp.int32).astype(F32) * s_ref[i, r]

    def phase(p):
        du, dd = T - 1 - p, p
        iu, idn = du - 1, dd

        def chunk(r, _):
            if p == 0:
                tok_copy(r).wait()

            @pl.when(t < du)
            def _():
                acc[rows(r), :] = product(du, r)

                @pl.when(has_lo)
                def _():
                    for c in u_copy(iu, r):
                        c.wait_recv()
                    acc[rows(r), :] += decode(ru, rsu, iu, r)

                encode(acc[rows(r), :], su, ssu, iu, r)
                for c in u_copy(iu, r):
                    c.start()

            if p == 0:
                @pl.when(r == 0)
                def _():
                    if order[1] != order[0]:
                        w_copy(order[1]).wait()

            @pl.when(t > dd)
            def _():
                acc[rows(r), :] = product(dd, r)

                @pl.when(has_hi)
                def _():
                    for c in d_copy(idn, r):
                        c.wait_recv()
                    acc[rows(r), :] += decode(rd, rsd, idn, r)

                encode(acc[rows(r), :], sd, ssd, idn, r)
                for c in d_copy(idn, r):
                    c.start()

            return 0

        lax.fori_loop(0, R, chunk, 0)

    def low_start():
        own_dn.wait()
        own_up.wait()
        for s in range(X - 1):
            for k in range(2):
                x_copy(s, k).wait_recv()
            for k in range(2):
                if s < X - 2:
                    x_copy(s + 1, k).start()
                c_copy(s + 1, k).start()
        for s in range(X):
            for k in range(2):
                c_copy(s, k).wait_recv()

        def block(b, _):
            slot = slot_of[apb[pos * NB + b]]
            at = pl.ds(pl.multiple_of(b * BL, BL), BL)
            low[b] = lax.dot_general(
                dn[slot], tok[at, :], (((1,), (1,)), ((), ())), preferred_element_type=F32)
            return 0

        lax.fori_loop(0, NB, block, 0)

        @pl.when(t == 0)
        def _():
            lsu[...] = low[...]
            low_up().start()

        @pl.when(t == T - 1)
        def _():
            lsd[...] = low[...]
            low_down().start()

    def low_up():
        return pltpu.make_async_remote_copy(
            src_ref=lsu, dst_ref=lru, send_sem=s_low.at[0], recv_sem=r_low.at[0],
            device_id={"tensor": t + 1}, device_id_type=MESH)

    def low_down():
        return pltpu.make_async_remote_copy(
            src_ref=lsd, dst_ref=lrd, send_sem=s_low.at[1], recv_sem=r_low.at[1],
            device_id={"tensor": t - 1}, device_id_type=MESH)

    def low_finish():
        @pl.when(has_lo)
        def _():
            low_up().wait_recv()

            @pl.when(has_hi)
            def _():
                lsu[...] = low[...] + lru[...]
                low_up().start()

        @pl.when(has_hi)
        def _():
            low_down().wait_recv()

            @pl.when(has_lo)
            def _():
                lsd[...] = low[...] + lrd[...]
                low_down().start()

            low[...] += lrd[...]

        @pl.when(has_lo)
        def _():
            low[...] += lru[...]

    waited = {order[0]}
    w_copy(order[0]).wait()
    for p in range(T - 1):
        if p == 0:
            waited.add(order[1])
        else:
            for d in (T - 1 - p, p):
                if d not in waited:
                    w_copy(d).wait()
                    waited.add(d)
        if p == T - 2:
            low_start()
        phase(p)

    def own(r, _):
        acc[rows(r), :] = product(t, r)
        return 0

    lax.fori_loop(0, R, own, 0)
    low_finish()

    def lora(b, _):
        slot = slot_of[apb[pos * NB + b]]
        at = pl.ds(pl.multiple_of(b * BL, BL), BL)
        whole = low[b]
        first = whole.astype(jnp.bfloat16)
        rest = whole - first.astype(F32)
        second = rest.astype(jnp.bfloat16)
        third = (rest - second.astype(F32)).astype(jnp.bfloat16)
        factor = up[slot]
        term = lax.dot_general(
            jnp.concatenate([first, second, third], axis=0),
            jnp.concatenate([factor] * 3, axis=0),
            (((0,), (0,)), ((), ())), preferred_element_type=F32)
        acc[at, :] += ADAPTER_SCALE * term
        return 0

    lax.fori_loop(0, NB, lora, 0)

    def finish(r, _):
        @pl.when(has_hi)
        def _():
            for c in d_copy(t, r):
                c.wait_recv()
            acc[rows(r), :] += decode(rd, rsd, t, r)

        @pl.when(has_lo)
        def _():
            for c in u_copy(t - 1, r):
                c.wait_recv()
            acc[rows(r), :] += decode(ru, rsu, t - 1, r)

        for j in range(RB // BL):
            b = r * (RB // BL) + j
            at = pl.ds(pl.multiple_of(b * BL, BL), BL)
            here = lax.broadcasted_iota(jnp.int32, (BL, N), 0) < live[b]
            out[at, :] = jnp.where(here, acc[at, :], 0.0).astype(out.dtype)
        return 0

    lax.fori_loop(0, R, finish, 0)

    for p in range(T - 1):
        du, dd = T - 1 - p, p

        def sent(r, _):
            @pl.when(t < du)
            def _():
                for c in u_copy(du - 1, r):
                    c.wait_send()

            @pl.when(t > dd)
            def _():
                for c in d_copy(dd, r):
                    c.wait_send()

            return 0

        lax.fori_loop(0, R, sent, 0)

    @pl.when(has_hi)
    def _():
        low_up().wait_send()

    @pl.when(has_lo)
    def _():
        low_down().wait_send()

    for k in range(2):
        for s in range(X - 1):
            x_copy(s, k).wait_send()
        for s in range(X):
            c_copy(s, k).wait_send()


def on_device(T, DP, tokens, weight, down, up, apb, live, slot_of):
    X = DP // 2
    M, K = tokens.shape
    N = weight.shape[1] // T
    NB = live.shape[0]
    BL = M // NB
    AP, RANK = down.shape[0], down.shape[2]
    A = AP * DP
    R = max(1, min(4, NB))
    down = jnp.swapaxes(down, 1, 2)
    bf16, i16 = jnp.bfloat16, jnp.int16
    D = max(T - 1, 1)
    V, DMA = pltpu.VMEM, pltpu.SemaphoreType.DMA
    smem = pl.BlockSpec(memory_space=pltpu.SMEM)
    hbm = pl.BlockSpec(memory_space=pl.ANY)
    scratch = (
        [V((M, K), bf16), V((T, K, N), bf16), V((A, RANK, K), bf16), V((A, RANK, N), bf16)]
        + [V((M, N), F32), V((NB, RANK, BL), F32)]
        + [V((D, M, N), i16)] * 4
        + [V((D, R, 1, N), F32)] * 4
        + [V((NB, RANK, BL), F32)] * 4
        + [DMA((R,)), DMA((T,)), DMA((2,))]
        + [DMA((D, R))] * 8
        + [DMA((2,)), DMA((2,))]
        + [DMA((max(X - 1, 1), 2)), DMA((max(X - 1, 1), 2)), DMA((X, 2)), DMA((X, 2))]
    )
    return pl.pallas_call(
        functools.partial(kernel, T, X, R, NB, BL),
        out_shape=jax.ShapeDtypeStruct((M, N), bf16),
        in_specs=[smem, smem, smem, hbm, hbm, hbm, hbm],
        out_specs=pl.BlockSpec(memory_space=pltpu.VMEM),
        scratch_shapes=scratch,
        compiler_params=pltpu.CompilerParams(
            collective_id=0, has_side_effects=True, vmem_limit_bytes=56 * 2**20),
        cost_estimate=pl.CostEstimate(
            flops=2 * M * K * N * T, bytes_accessed=2 * (M * K + K * N * T), transcendentals=0),
    )(apb, slot_of, live, tokens, weight, down, up)


def solution(mesh):
    placed = (
        P(("groups", "dp"), "tensor"),
        P("tensor", None),
        P(("groups", "dp"), "tensor", None),
        P(("groups", "dp"), None, "tensor"),
        P("groups"),
        P(("groups", "dp")),
        P("groups"),
    )
    return jax.shard_map(
        functools.partial(on_device, mesh.shape["tensor"], mesh.shape["dp"]),
        mesh=mesh,
        in_specs=placed,
        out_specs=P(("groups", "dp"), "tensor"),
        check_vma=False,
    )
```

time: 273 us -> 108 us (0.40)
  waiting for transfers between devices: 228 us -> 0 us
  Pallas kernels: 0 us -> 105 us
  matrix products: 21.4 us -> 0 us
  between operations: 13.2 us -> 0.01 us
  local copies, waits for them, and re-layouts: 6.78 us -> 2.26 us
  other arithmetic: 3.76 us -> 0 us
    reduce_scatter x1 -> x0, waiting for transfers between devices: 145 us -> none  [on_device(): lax.psum_scatter(base_output, 'tensor', scatter_dimension=1, tiled=True)]
    pallas_call x0 -> x1, Pallas kernels: none -> 105 us  [on_device(): pl.pallas_call(functools.partial(kernel, T, X, R, NB, BL), out_shape=jax....]
    all_gather x2 -> x0, waiting for transfers between devices: 48.4 us -> none  [the longest x1 48.4 us: on_device(): lax.all_gather(adapter_down_factors, 'dp', axis=0, tiled=True)]
    psum x1 -> x0, waiting for transfers between devices: 33.3 us -> none  [on_device(): low_whole = lax.psum(lowrank_output, 'tensor')]
    dot_general x3 -> x0, matrix products: 21.4 us -> none  [the longest x1 14.8 us: on_device(): jnp.dot(tokens, key_value_weight, preferred_element_type=jnp.float32)]
    gather x3 -> x0, local copies, waits for them, and re-layouts: 6.15 us -> none  [the longest x1 3.46 us: on_device(): pieces[0][piece_index]]
    convert_element_type x1 -> x0, other arithmetic: 2.85 us -> none  [on_device(): return result.astype(jnp.bfloat16)]
  transfers between devices with their start and end apart: 4 -> 0, of which waited for: 3 -> 0; matrix products, arithmetic and copies ran while one was open for 10% -> 0% of each run, Pallas kernels for 0% -> 0%
where the time goes in v1:
time: 108 us
  Pallas kernels  105 us (97%)
  local copies, waits for them, and re-layouts  2.26 us (2%)
    pallas_call x1, Pallas kernels, on_device(): pl.pallas_call(functools.partial(kernel, T, X, R, NB, BL), out_shape=jax....  105 us
    unnamed x1, local copies, waits for them, and re-layouts  2.26 us

profile of v1, /device:TPU:0, one launch (start us, length us, event | category | flops | bytes accessed | tf_op | source)
XLA Modules:
  0.0 107.6 jit_solution(9678664503071654567)
XLA Ops:
  0.0 105.3 %shard_map.73 = bf16[1024,512]{1,0:T(8,128)(2,1)} custom-call(s32[32]{0:T(128)} %apb.1, s32[24]{0:T(128)} %slot_of.1, s32[8]{0:T(128)} %live.1, bf16[1024,2048]{1,0:T(8,128)(2,1)} %tok_h.1, bf16[2048,2048]{1,0:T(8,128)(2,1)} %w_h.1, bf16[6,64,2048]{2,1,0:T(8,128)(2,1)} %bitcast.1, bf16[6,64,512]{2,1,0:T(8,128)(2,1)} %up_h.1), custom_call_target="tpu_custom_call" | custom-call | flops 8589934592 | bytes 12582912 | tf_op jit(solution)/shard_map/pallas_call | solution.py:374
  105.3 2.3 %copy.9 = bf16[1024,512]{1,0:T(8,128)(2,1)} copy(bf16[1024,512]{1,0:T(8,128)(2,1)} %shard_map.73) | data formatting | bytes 2097152

commit v2 on v1

--- a/solution.py
+++ b/solution.py
@@ -11,14 +11,16 @@
 MESH = pl.DeviceIdType.MESH
 F32 = jnp.float32
 LEVELS = 32767.0
+AHEAD = 2
+LAG = 2
 
 
 def kernel(
     T, X, R, NB, BL,
     apb, slot_of, live, tok_h, w_h, dn_h, up_h, out,
-    tok, w, dn, up, acc, low,
+    tok, w, dn, up, acc, hold, low,
     su, sd, ru, rd, ssu, ssd, rsu, rsd,
-    lsu, lsd, lru, lrd,
+    lsu, lsd, lru, lrd, slu, sld, rlu, rld,
     sem_tok, sem_w, sem_own,
     s_u, s_d, r_u, r_d, s_us, s_ds, r_us, r_ds,
     s_low, r_low, s_x, r_x, s_c, r_c,
@@ -49,22 +51,42 @@
     def tok_copy(r):
         return pltpu.make_async_copy(tok_h.at[rows(r)], tok.at[rows(r)], sem_tok.at[r])
 
-    w_copy(order[0]).start()
+    lower = t < T // 2
+    upper = jnp.logical_not(lower)
+    lag_u = LAG * upper.astype(jnp.int32)
+    lag_d = LAG - lag_u
+
+    @pl.when(lower)
+    def _():
+        w_copy(T - 1).start()
+
+    @pl.when(upper)
+    def _():
+        w_copy(0).start()
+
     tok_copy(0).start()
-    w_copy(order[1]).start()
-    for r in range(1, R):
-        tok_copy(r).start()
-    for d in order[2:]:
-        w_copy(d).start()
+
+    def load_rest():
+        @pl.when(lower)
+        def _():
+            w_copy(0).start()
+
+        @pl.when(upper)
+        def _():
+            w_copy(T - 1).start()
+
+        for r in range(1, R):
+            tok_copy(r).start()
+        for d in order[2:]:
+            w_copy(d).start()
+        own_dn.start()
+        own_up.start()
 
     def piece(ref, owner):
         return ref.at[pl.ds(owner * AP, AP)]
 
     own_dn = pltpu.make_async_copy(dn_h, piece(dn, pos), sem_own.at[0])
     own_up = pltpu.make_async_copy(up_h, piece(up, pos), sem_own.at[1])
-    own_dn.start()
-    own_up.start()
-
     bar = pltpu.get_barrier_semaphore()
 
     @pl.when(has_lo)
@@ -82,8 +104,6 @@
         peers.append(left)
     for q in peers:
         pl.semaphore_signal(bar, inc=1, device_id={"dp": q}, device_id_type=MESH)
-    pl.semaphore_wait(bar, has_lo.astype(jnp.int32) + has_hi.astype(jnp.int32) + len(peers))
-
     def x_copy(s, k):
         owner = lax.rem(x - s + X, X) * 2 + core
         full, mine = (dn, dn_h) if k == 0 else (up, up_h)
@@ -100,11 +120,12 @@
             send_sem=s_c.at[s, k], recv_sem=r_c.at[s, k],
             device_id={"dp": partner}, device_id_type=MESH)
 
-    if X > 1:
+    def gather_start():
+        if X > 1:
+            for k in range(2):
+                x_copy(0, k).start()
         for k in range(2):
-            x_copy(0, k).start()
-    for k in range(2):
-        c_copy(0, k).start()
+            c_copy(0, k).start()
 
     def u_copy(i, r):
         return (
@@ -137,51 +158,119 @@
     def decode(q_ref, s_ref, i, r):
         return q_ref[i, rows(r), :].astype(jnp.int32).astype(F32) * s_ref[i, r]
 
+    def before_up(p, r):
+        for c in u_copy(T - 2 - p, r):
+            c.wait_send()
+
+    def before_down(p, r):
+        for c in d_copy(p, r):
+            c.wait_send()
+
+    def throttle(p, r, before):
+        @pl.when(r >= AHEAD)
+        def _():
+            before(p, r - AHEAD)
+
+        if p > 0:
+            @pl.when(r < AHEAD)
+            def _():
+                before(p - 1, r + R - AHEAD)
+
     def phase(p):
         du, dd = T - 1 - p, p
         iu, idn = du - 1, dd
 
-        def chunk(r, _):
-            if p == 0:
-                tok_copy(r).wait()
-
-            @pl.when(t < du)
-            def _():
-                acc[rows(r), :] = product(du, r)
-
+        def step(k, first):
+            u, d = k - lag_u, k - lag_d
+            up_on = (t < du) & (u >= 0) & (u < R)
+            down_on = (t > dd) & (d >= 0) & (d < R)
+            if first:
+                tok_copy(0).wait()
+
+                @pl.when(lower)
+                def _():
+                    w_copy(du).wait()
+
+                @pl.when(upper)
+                def _():
+                    w_copy(dd).wait()
+
+                load_rest()
+            elif p == 0:
+                @pl.when(k < R)
+                def _():
+                    tok_copy(k).wait()
+
+            @pl.when(up_on)
+            def _():
+                acc[rows(u), :] = product(du, u)
+
+                @pl.when(t == 0)
+                def _():
+                    encode(acc[rows(u), :], su, ssu, iu, u)
+
+            @pl.when(down_on)
+            def _():
+                hold[...] = product(dd, d)
+
+                @pl.when(t == T - 1)
+                def _():
+                    encode(hold[...], sd, ssd, idn, d)
+
+            if first:
+                pl.semaphore_wait(
+                    bar, has_lo.astype(jnp.int32) + has_hi.astype(jnp.int32) + len(peers))
+                gather_start()
+
+            @pl.when(up_on)
+            def _():
                 @pl.when(has_lo)
                 def _():
-                    for c in u_copy(iu, r):
+                    for c in u_copy(iu, u):
                         c.wait_recv()
-                    acc[rows(r), :] += decode(ru, rsu, iu, r)
-
-                encode(acc[rows(r), :], su, ssu, iu, r)
-                for c in u_copy(iu, r):
+                    encode(acc[rows(u), :] + decode(ru, rsu, iu, u), su, ssu, iu, u)
+
+                throttle(p, u, before_up)
+                for c in u_copy(iu, u):
                     c.start()
 
-            if p == 0:
-                @pl.when(r == 0)
-                def _():
-                    if order[1] != order[0]:
-                        w_copy(order[1]).wait()
-
-            @pl.when(t > dd)
-            def _():
-                acc[rows(r), :] = product(dd, r)
-
+            @pl.when(down_on)
+            def _():
                 @pl.when(has_hi)
                 def _():
-                    for c in d_copy(idn, r):
+                    for c in d_copy(idn, d):
                         c.wait_recv()
-                    acc[rows(r), :] += decode(rd, rsd, idn, r)
-
-                encode(acc[rows(r), :], sd, ssd, idn, r)
-                for c in d_copy(idn, r):
+                    encode(hold[...] + decode(rd, rsd, idn, d), sd, ssd, idn, d)
+
+                throttle(p, d, before_down)
+                for c in d_copy(idn, d):
                     c.start()
 
+            if p == T - 2:
+                @pl.when((u == 0) & (t == 0))
+                def _():
+                    for c in low_up():
+                        c.wait_send()
+
+                @pl.when((d == 0) & (t == T - 1))
+                def _():
+                    for c in low_down():
+                        c.wait_send()
+
+            if first:
+                @pl.when(lower & has_lo)
+                def _():
+                    w_copy(dd).wait()
+
+                @pl.when(upper & has_hi)
+                def _():
+                    w_copy(du).wait()
+
             return 0
 
-        lax.fori_loop(0, R, chunk, 0)
+        if p == 0:
+            step(0, True)
+        lax.fori_loop(1 if p == 0 else 0, R + LAG, lambda k, _: step(k, False), 0)
 
     def low_start():
         own_dn.wait()
@@ -204,66 +293,80 @@
                 dn[slot], tok[at, :], (((1,), (1,)), ((), ())), preferred_element_type=F32)
             return 0
 
+
         lax.fori_loop(0, NB, block, 0)
 
         @pl.when(t == 0)
         def _():
-            lsu[...] = low[...]
-            low_up().start()
+            low_send(low[...], lsu, slu, low_up())
 
         @pl.when(t == T - 1)
         def _():
-            lsd[...] = low[...]
-            low_down().start()
+            low_send(low[...], lsd, sld, low_down())
+
+    def low_copies(src, dst, scale_src, scale_dst, at, target):
+        return [
+            pltpu.make_async_remote_copy(
+                src_ref=a, dst_ref=b, send_sem=s_low.at[at, k], recv_sem=r_low.at[at, k],
+                device_id={"tensor": target}, device_id_type=MESH)
+            for k, (a, b) in enumerate([(src, dst), (scale_src, scale_dst)])
+        ]
 
     def low_up():
-        return pltpu.make_async_remote_copy(
-            src_ref=lsu, dst_ref=lru, send_sem=s_low.at[0], recv_sem=r_low.at[0],
-            device_id={"tensor": t + 1}, device_id_type=MESH)
+        return low_copies(lsu, lru, slu, rlu, 0, t + 1)
 
     def low_down():
-        return pltpu.make_async_remote_copy(
-            src_ref=lsd, dst_ref=lrd, send_sem=s_low.at[1], recv_sem=r_low.at[1],
-            device_id={"tensor": t - 1}, device_id_type=MESH)
+        return low_copies(lsd, lrd, sld, rld, 1, t - 1)
+
+    def low_send(v, q_ref, s_ref, copies):
+        top = jnp.maximum(jnp.max(jnp.abs(v), axis=1, keepdims=True), 1e-30)
+        q_ref[...] = jnp.round(v * (LEVELS / top)).astype(jnp.int32).astype(jnp.int16)
+        s_ref[...] = top * (1.0 / LEVELS)
+        for c in copies:
+            c.start()
+
+    def low_decode(q_ref, s_ref):
+        return q_ref[...].astype(jnp.int32).astype(F32) * s_ref[...]
 
     def low_finish():
         @pl.when(has_lo)
         def _():
-            low_up().wait_recv()
+            for c in low_up():
+                c.wait_recv()
 
             @pl.when(has_hi)
             def _():
-                lsu[...] = low[...] + lru[...]
-                low_up().start()
+                low_send(low[...] + low_decode(lru, rlu), lsu, slu, low_up())
 
         @pl.when(has_hi)
         def _():
-            low_down().wait_recv()
+            for c in low_down():
+                c.wait_recv()
 
             @pl.when(has_lo)
             def _():
-                lsd[...] = low[...] + lrd[...]
-                low_down().start()
-
-            low[...] += lrd[...]
+                low_send(low[...] + low_decode(lrd, rld), lsd, sld, low_down())
+
+            low[...] += low_decode(lrd, rld)
 
         @pl.when(has_lo)
         def _():
-            low[...] += lru[...]
-
-    waited = {order[0]}
-    w_copy(order[0]).wait()
+            low[...] += low_decode(lru, rlu)
+
+    waited = {0, T - 1}
     for p in range(T - 1):
-        if p == 0:
-            waited.add(order[1])
-        else:
-            for d in (T - 1 - p, p):
-                if d not in waited:
-                    w_copy(d).wait()
-                    waited.add(d)
+        for d in (T - 1 - p, p):
+            if d not in waited:
+                w_copy(d).wait()
+                waited.add(d)
         if p == T - 2:
             low_start()
         phase(p)
+
+    for d in (0, T - 1):
+        @pl.when(t == d)
+        def _():
+            w_copy(d).wait()
 
     def own(r, _):
         acc[rows(r), :] = product(t, r)
@@ -312,31 +415,22 @@
 
     lax.fori_loop(0, R, finish, 0)
 
-    for p in range(T - 1):
-        du, dd = T - 1 - p, p
-
-        def sent(r, _):
-            @pl.when(t < du)
-            def _():
-                for c in u_copy(du - 1, r):
-                    c.wait_send()
-
-            @pl.when(t > dd)
-            def _():
-                for c in d_copy(dd, r):
-                    c.wait_send()
-
-            return 0
-
-        lax.fori_loop(0, R, sent, 0)
-
     @pl.when(has_hi)
     def _():
-        low_up().wait_send()
+        for j in range(AHEAD):
+            for c in u_copy(t, R - AHEAD + j):
+                c.wait_send()
 
     @pl.when(has_lo)
     def _():
-        low_down().wait_send()
+        for j in range(AHEAD):
+            for c in d_copy(t - 1, R - AHEAD + j):
+                c.wait_send()
+
+    @pl.when(has_lo & has_hi)
+    def _():
+        for c in low_up() + low_down():
+            c.wait_send()
 
     for k in range(2):
         for s in range(X - 1):
@@ -362,13 +456,14 @@
     hbm = pl.BlockSpec(memory_space=pl.ANY)
     scratch = (
         [V((M, K), bf16), V((T, K, N), bf16), V((A, RANK, K), bf16), V((A, RANK, N), bf16)]
-        + [V((M, N), F32), V((NB, RANK, BL), F32)]
+        + [V((M, N), F32), V((M // R, N), F32), V((NB, RANK, BL), F32)]
         + [V((D, M, N), i16)] * 4
         + [V((D, R, 1, N), F32)] * 4
-        + [V((NB, RANK, BL), F32)] * 4
+        + [V((NB, RANK, BL), i16)] * 4
+        + [V((NB, 1, BL), F32)] * 4
         + [DMA((R,)), DMA((T,)), DMA((2,))]
         + [DMA((D, R))] * 8
-        + [DMA((2,)), DMA((2,))]
+        + [DMA((2, 2)), DMA((2, 2))]
         + [DMA((max(X - 1, 1), 2)), DMA((max(X - 1, 1), 2)), DMA((X, 2)), DMA((X, 2))]
     )
     return pl.pallas_call(

time: 108 us -> 86.5 us (0.80)
  Pallas kernels: 105 us -> 82.8 us
    pallas_call x1, Pallas kernels: 105 us -> 82.8 us  [on_device(): pl.pallas_call(functools.partial(kernel, T, X, R, NB, BL), out_shape=jax....]
where the time goes in v2:
time: 86.5 us; the launch traced here: 85.1 us
  Pallas kernels  82.8 us (96%)
  local copies, waits for them, and re-layouts  2.26 us (3%)
    pallas_call x1, Pallas kernels, on_device(): pl.pallas_call(functools.partial(kernel, T, X, R, NB, BL), out_shape=jax....  82.8 us
    unnamed x1, local copies, waits for them, and re-layouts  2.26 us

profile of v2, /device:TPU:0, one launch (start us, length us, event | category | flops | bytes accessed | tf_op | source)
XLA Modules:
  0.0 85.1 jit_solution(7211643736883166125)
XLA Ops:
  0.0 82.8 %shard_map.73 = bf16[1024,512]{1,0:T(8,128)(2,1)} custom-call(s32[32]{0:T(128)} %apb.1, s32[24]{0:T(128)} %slot_of.1, s32[8]{0:T(128)} %live.1, bf16[1024,2048]{1,0:T(8,128)(2,1)} %tok_h.1, bf16[2048,2048]{1,0:T(8,128)(2,1)} %w_h.1, bf16[6,64,2048]{2,1,0:T(8,128)(2,1)} %bitcast.1, bf16[6,64,512]{2,1,0:T(8,128)(2,1)} %up_h.1), custom_call_target="tpu_custom_call" | custom-call | flops 8589934592 | bytes 12582912 | tf_op jit(solution)/shard_map/pallas_call | solution.py:469
  82.9 2.3 %copy.9 = bf16[1024,512]{1,0:T(8,128)(2,1)} copy(bf16[1024,512]{1,0:T(8,128)(2,1)} %shard_map.73) | data formatting | bytes 2097152
